TPU v7x, 32 devices: a whole 2x2x4 slice. The times are simulated.
32 devices in a mesh: groups: 2 (over y), expert: 16 (over z, x, core).
Axes of the slice: x: 2, y: 2, z: 4, core: 2. Of those that a mesh axis runs over, the one named last changes fastest.
Arguments:
- attn_heads: bfloat16 [4096, 4096], P(('groups', 'expert')), parts along dimension 0, may hold values from -6 to 6
- residual: bfloat16 [4096, 2048], P(('groups', 'expert')), parts along dimension 0, may hold values from -6 to 6
- w_out: bfloat16 [4096, 2048], P('expert'), may hold values from -0.09375 to 0.09375
- norm_gain: float32 [2048], replicated, may hold values from 0.1 to 1.9
- expert_ids: int32 [4096, 8], P(('groups', 'expert')), parts along dimension 0, may hold values from 0 to 15, all different within a row; in each aligned block of 128 rows (0 to 127, 128 to 255, ...) at most 80 rows name the same one
- route_num: int32 [4096, 8], P(('groups', 'expert')), parts along dimension 0, may hold values from 1 to 16
- w_gate: bfloat16 [16, 2048, 768], P('expert'), may hold values from -0.125 to 0.125
- w_up: bfloat16 [16, 2048, 768], P('expert'), may hold values from -0.125 to 0.125
- w_down: bfloat16 [16, 768, 2048], P('expert'), may hold values from -0.21875 to 0.21875
Outputs:
- mid_state: bfloat16 [4096, 2048], P(('groups', 'expert')), parts along dimension 0
- expert_out: bfloat16 [4096, 2048], P(('groups', 'expert')), parts along dimension 0
There are 2 independent parts, one for each index of `groups`. A program takes and returns all parts, laid end to end along the dimension named above; an argument that names none is the same for every part. Nothing has to cross between parts.
Inputs may be any that keep to these rules, and one draw needn't show every extreme that they name: `expert_ids`: each token names 8 different experts; among the 128 tokens of one device no expert is named more than 80 times, a bound that some block reaches.
All inputs are finite; a program needn't handle non-finite values.
Results may differ from a plain program's by a relative error of at most 0.0095.
Values may be sent and summed in bfloat16 or wider, within the bound.
A program may use at most 128 MiB of HBM per device.

v0:
```python
import jax
import jax.numpy as jnp
from jax import lax
from jax.sharding import PartitionSpec as P

epsilon = 1e-06


def rms_scale(tensor, norm_gain):
    values = tensor.astype(jnp.float32)
    mean_sq = jnp.mean(values * values, axis=-1, keepdims=True)
    return (values * lax.rsqrt(mean_sq + epsilon) * norm_gain).astype(jnp.bfloat16)


def per_device(attn_heads, residual, w_out, norm_gain, expert_ids, route_num, w_gate, w_up, w_down):
    tok_rows = attn_heads.shape[0]
    feature_count = residual.shape[1]
    gathered = lax.all_gather(w_out, "expert", axis=0, tiled=True)
    projected = jnp.dot(attn_heads, gathered, preferred_element_type=jnp.float32)
    mid_state = (residual.astype(jnp.float32) + projected).astype(jnp.bfloat16)
    n_experts = lax.axis_size("expert")
    top_count = expert_ids.shape[1]
    capacity = tok_rows * top_count * 5 // (4 * n_experts)
    flat_ids = expert_ids.reshape(-1)
    onehot = (flat_ids[:, None] == jnp.arange(n_experts, dtype=jnp.int32)[None, :]).astype(
        jnp.int32
    )
    before = jnp.cumsum(onehot, axis=0) - onehot
    slot_index = jnp.sum(before * onehot, axis=1)
    position = flat_ids * capacity + slot_index
    token_index = jnp.arange(tok_rows * top_count, dtype=jnp.int32) // top_count
    payload = rms_scale(mid_state, norm_gain)
    sendbuf = jnp.zeros((n_experts * capacity, feature_count), jnp.bfloat16)
    sendbuf = sendbuf.at[position].set(payload[token_index])
    sendbuf = sendbuf.reshape(n_experts, capacity, feature_count)
    received = lax.all_to_all(sendbuf, "expert", split_axis=0, concat_axis=0, tiled=True)
    sources, slot_count, _ = received.shape
    row_block = received.reshape(sources * slot_count, feature_count)
    gate_act = jnp.dot(row_block, w_gate[0], preferred_element_type=jnp.float32)
    up_act = jnp.dot(row_block, w_up[0], preferred_element_type=jnp.float32)
    hidden = (jax.nn.silu(gate_act) * up_act).astype(jnp.bfloat16)
    result = jnp.dot(hidden, w_down[0], preferred_element_type=jnp.float32).astype(jnp.bfloat16)
    result = result.reshape(sources, slot_count, feature_count)
    returned = lax.all_to_all(result, "expert", split_axis=0, concat_axis=0, tiled=True)
    returned = returned.reshape(n_experts * capacity, feature_count)
    picked = returned[position].astype(jnp.float32).reshape(tok_rows, top_count, feature_count)
    numer = route_num.astype(jnp.float32)
    weights = numer / jnp.sum(numer, axis=1, keepdims=True)
    expert_out = jnp.sum(picked * weights[:, :, None], axis=1).astype(jnp.bfloat16)
    return (mid_state, expert_out)


def solution(mesh):
    in_specs = (
        P(("groups", "expert"), None),
        P(("groups", "expert"), None),
        P("expert", None),
        P(),
        P(("groups", "expert"), None),
        P(("groups", "expert"), None),
        P("expert", None, None),
        P("expert", None, None),
        P("expert", None, None),
    )
    out_specs = (P(("groups", "expert"), None), P(("groups", "expert"), None))
    return jax.shard_map(
        per_device, mesh=mesh, in_specs=in_specs, out_specs=out_specs, check_vma=False
    )
```

profile of v0, /device:TPU:25, one launch (start us, length us, event | category | flops | bytes accessed | tf_op | source)
XLA Modules:
  0.0 445.4 jit_solution(2157559371774095986)
XLA Ops:
  7.2 0.7 all-gather.2.cloned.1.call-update
  7.9 1.0 copy.15
  8.9 0.1 eq.29
  9.0 0.1 eq.25
  9.1 0.7 broadcast_multiply_fusion
  9.8 0.1 copy.14
  9.9 0.1 mul.55
  10.0 4.5 %reduce-window.6 = s32[16,8,128]{2,1,0:T(8,128)S(1)} reduce-window(s32[16,8,128]{2,1,0:T(8,128)S(1)} %fusion.16, s32[]{:T(128)} %constant.31.clone.1), window={size=1x1x128 pad=0_0x0_0x127_0}, to_apply=%region_0.0 | reduce-window | flops 2080768 | bytes 131076 | tf_op jit(solution)/shard_map/reduce-window
  14.6 0.1 copy.17
  14.8 0.1 broadcast_add_fusion
  15.0 121.6 %all-gather.2.cloned.1.call-done = bf16[4096,2048]{1,0:T(8,128)(2,1)} async-done(((bf16[256,2048]{1,0:T(8,128)(2,1)}), bf16[4096,2048]{1,0:T(8,128)(2,1)}) %all-gather.2.cloned.1.call-update) | async-done | bytes 16777232 | tf_op jit(solution)/shard_map/all_gather | solution.py:18
  136.6 8.6 %fusion.10 = (f32[128]{0:T(128)S(1)}, bf16[128,2048]{1,0:T(8,128)(2,1)S(1)}) fusion(bf16[128,4096]{1,0:T(8,128)(2,1)} %param.9, bf16[4096,2048]{1,0:T(8,128)(2,1)} %all-gather.2.cloned.1.call-done, bf16[128,2048]{1,0:T(8,128)(2,1)} %param.10), kind=kOutput, calls=%fused_computation.19 | convolution fusion | flops 2149056512 | bytes 18874880 | tf_op jit(solution)/shard_map/dot_general | solution.py:19
  145.2 0.8 copy-done.1
  146.0 1.0 fusion.12
  147.0 23.5 %scatter_custom_fusion = bf16[1280,2048]{1,0:T(8,128)(2,1)} fusion(s32[1024]{0:T(1024)S(1)} %bitcast.50, bf16[128,2048]{1,0:T(8,128)(2,1)} %fusion.12, s32[1024]{0:T(1024)S(1)} %broadcast_clamp_fusion.1, bf16[]{:T(256)} %constant.29.clone.1), kind=kCustom, calls=%fused_computation.6 | custom fusion | bytes 5243392 | tf_op jit(solution)/shard_map/scatter | solution.py:34
  170.5 120.0 %all_to_all.10 = bf16[16,80,2048]{2,1,0:T(8,128)(2,1)S(1)} all-to-all(bf16[16,80,2048]{2,1,0:T(8,128)(2,1)} %bitcast.43), channel_id=1, replica_groups=mesh['groups'=2,'expert'=16] {'expert'}, dimensions={0} | all-to-all | bytes 10485760 | tf_op jit(solution)/shard_map/all_to_all | solution.py:36
  290.4 4.3 fusion.6
  294.8 4.8 %fusion.3 = bf16[1280,768]{1,0:T(8,128)(2,1)S(1)} fusion(bf16[1280,2048]{1,0:T(8,128)(2,1)S(1)} %bitcast.46, f32[1280,768]{1,0:T(8,128)S(1)} %fusion.6, bf16[1,2048,768]{2,1,0:T(8,128)(2,1)S(1)} %copy-done.5), kind=kOutput, calls=%fused_computation.9 | convolution fusion | flops 4032430080 | bytes 14286848 | tf_op jit(solution)/shard_map/dot_general | solution.py:40
  299.6 6.1 %convolution_convert_fusion = bf16[1280,2048]{1,0:T(8,128)(2,1)} fusion(bf16[1280,768]{1,0:T(8,128)(2,1)S(1)} %fusion.3, bf16[1,768,2048]{2,1,0:T(8,128)(2,1)S(1)} %copy-done), kind=kOutput, calls=%fused_computation.5 | convolution fusion | flops 4029153280 | bytes 10354688 | tf_op jit(solution)/shard_map/dot_general | solution.py:42
  305.7 6.1 %all-to-all-start.1 = ((bf16[16,80,2048]{2,1,0:T(8,128)(2,1)}), bf16[16,80,2048]{2,1,0:T(8,128)(2,1)}, u32[]{:S(2)}, u32[]{:S(2)}) async-start(bf16[16,80,2048]{2,1,0:T(8,128)(2,1)} %bitcast.44), calls=%async_computation.1 | async-start | bytes 10485760 | tf_op jit(solution)/shard_map/all_to_all | solution.py:44
  311.8 0.1 copy.19
  311.9 107.3 %all-to-all-done.1 = bf16[16,80,2048]{2,1,0:T(8,128)(2,1)} async-done(((bf16[16,80,2048]{2,1,0:T(8,128)(2,1)}), bf16[16,80,2048]{2,1,0:T(8,128)(2,1)}, u32[]{:S(2)}, u32[]{:S(2)}) %all-to-all-start.1) | async-done | bytes 5242912 | tf_op jit(solution)/shard_map/all_to_all | solution.py:44
  419.2 12.0 %gather_fusion = bf16[1024,2048]{1,0:T(8,128)(2,1)} fusion(bf16[1280,2048]{1,0:T(8,128)(2,1)} %bitcast.11, s32[1024]{0:T(1024)S(1)} %broadcast_clamp_fusion), kind=kCustom, calls=%fused_computation.1 | custom fusion | bytes 8392704 | tf_op jit(solution)/shard_map/gather | solution.py:46
  431.3 7.3 %fusion = bf16[128,2048]{1,0:T(8,128)(2,1)} fusion(bf16[1024,2048]{1,0:T(8,128)(2,1)} %gather_fusion, f32[128,8]{1,0:T(8,128)S(1)} %copy.19), kind=kLoop, calls=%fused_computation.4 | loop fusion | flops 6029312 | bytes 4722688 | tf_op jit(solution)/shard_map/reduce_sum | solution.py:49
  (25 shorter events, 0.3 us)
Async XLA Ops:
  7.2 292.4 %copy-start = (bf16[1,768,2048]{2,1,0:T(8,128)(2,1)S(1)}, bf16[1,768,2048]{2,1,0:T(8,128)(2,1)}, u32[]{:S(2)}) copy-start(bf16[1,768,2048]{2,1,0:T(8,128)(2,1)} %param.17) | copy-start | bytes 9437188
  7.2 129.4 %all-gather.2.cloned.1.call-start = ((), (), s32[]{:S(2)}) async-start(), calls=%async_computation.2 | async-start | bytes 17825792 | tf_op jit(solution)/shard_map/all_gather | solution.py:18
  15.0 131.0 %copy-start.3 = (f32[2048]{0:T(1024)S(1)}, f32[2048]{0:T(1024)}, u32[]{:S(2)}) copy-start(f32[2048]{0:T(1024)} %param.12) | copy-start | bytes 24580
  145.2 0.8 copy-start.1
  170.5 120.0 %copy-start.4 = (bf16[1,2048,768]{2,1,0:T(8,128)(2,1)S(1)}, bf16[1,2048,768]{2,1,0:T(8,128)(2,1)}, u32[]{:S(2)}) copy-start(bf16[1,2048,768]{2,1,0:T(8,128)(2,1)} %param.15) | copy-start | bytes 9437188
  290.4 4.3 copy-start.5
  305.7 6.1 %copy-start.2 = (s32[128,8]{0,1:T(8,128)S(1)}, s32[128,8]{0,1:T(8,128)}, u32[]{:S(2)}) copy-start(s32[128,8]{0,1:T(8,128)} %param.14) | copy-start | bytes 12292
  305.7 113.6 %all-to-all-start.1 = ((bf16[16,80,2048]{2,1,0:T(8,128)(2,1)}), bf16[16,80,2048]{2,1,0:T(8,128)(2,1)}, u32[]{:S(2)}, u32[]{:S(2)}) async-start(bf16[16,80,2048]{2,1,0:T(8,128)(2,1)} %bitcast.44), calls=%async_computation.1 | async-start | bytes 10485760 | tf_op jit(solution)/shard_map/all_to_all | solution.py:44
Sparse Core Ops, SparseCore 0:
  10.2 126.3 all-gather.1
where the time goes:
time: 454 us; the launch traced here: 445 us
  waiting for transfers between devices  230 us (51%)
  blocking collectives  120 us (26%)
  local copies, waits for them, and re-layouts  38.1 us (8%)
  matrix products  23.8 us (5%)
  between operations  14.2 us (3%)
  other arithmetic  13.7 us (3%)
  starting transfers between devices  6.16 us (1%)
    all_gather x1, waiting for transfers between devices, per_device(): gathered = lax.all_gather(w_out, 'expert', axis=0, tiled=True)  122 us
    all_to_all x1, blocking collectives, per_device(): lax.all_to_all(sendbuf, 'expert', split_axis=0, concat_axis=0, tiled=True)  120 us
    all_to_all x1, waiting for transfers between devices, per_device(): lax.all_to_all(result, 'expert', split_axis=0, concat_axis=0, tiled=True)  107 us
    scatter x1, local copies, waits for them, and re-layouts, per_device(): sendbuf = sendbuf.at[position].set(payload[token_index])  23.5 us
    gather x1, local copies, waits for them, and re-layouts, per_device(): returned[position].astype(jnp.float32)  12 us
  transfers between devices with their start and end apart: 2, of which 2 were waited for; matrix products, arithmetic and copies ran while one was open for 2% of the time, Pallas kernels for 0%

commit v1 on v0

v1 whole, which is shorter than its diff:
```python
import functools

import jax
import jax.numpy as jnp
from jax import lax
from jax.experimental import pallas as pl
from jax.experimental.pallas import tpu as pltpu
from jax.sharding import PartitionSpec as P

epsilon = 1e-06
MESH = pl.DeviceIdType.MESH
F32, BF16 = jnp.float32, jnp.bfloat16
VMEM_BYTES = 56 * 1024 * 1024
DMA, VM = pltpu.SemaphoreType.DMA, pltpu.VMEM


def rms_scale(tensor, norm_gain):
    values = tensor.astype(F32)
    mean_sq = jnp.mean(values * values, axis=-1, keepdims=True)
    return (values * lax.rsqrt(mean_sq + epsilon) * norm_gain).astype(BF16)


def tile(size, most):
    return next(t for t in range(min(size, most), 0, -1) if size % t == 0 and (t % 128 == 0 or t == size))


class Place:
    def __init__(self, depth):
        e = lax.axis_index("expert")
        self.depth = depth
        self.z, self.x, self.c = e // 4, (e // 2) % 2, e % 2

    def back(self, k):
        return lax.rem(self.z + self.depth - k, self.depth)

    def at(self, z=None, x=None, c=None):
        z = self.z if z is None else z
        x = self.x if x is None else x
        c = self.c if c is None else c
        return {"expert": (z * 2 + x) * 2 + c}

    def others(self):
        targets = [self.at(z=lax.rem(self.z + k, self.depth)) for k in range(1, self.depth)]
        return targets + [self.at(x=1 - self.x), self.at(c=1 - self.c)]


def greet(targets):
    barrier = pltpu.get_barrier_semaphore()
    for target in targets:
        pl.semaphore_signal(barrier, inc=1, device_id=target, device_id_type=MESH)
    pl.semaphore_wait(barrier, len(targets))


def push(src, dst, sems, i, target):
    copy = pltpu.make_async_remote_copy(
        src_ref=src, dst_ref=dst, send_sem=sems[0].at[i], recv_sem=sems[1].at[i], device_id=target, device_id_type=MESH
    )
    copy.start()
    return copy


class Gather:
    def __init__(self, place, slot, zs, xs, cs):
        self.p, self.slot, self.zs, self.xs, self.cs = place, slot, zs, xs, cs
        self.sent = []

    def start(self):
        p = self.p
        own = self.slot(p.z, p.x, p.c)
        self.landed = {}
        for k in range(1, p.depth):
            self.sent.append(push(own, own, self.zs, k, p.at(z=lax.rem(p.z + k, p.depth))))
        self.x_on(0)
        self.c_on(0, p.z, p.x)

    def x_on(self, k):
        p = self.p
        ref = self.slot(p.back(k), p.x, p.c)
        self.sent.append(push(ref, ref, self.xs, k, p.at(x=1 - p.x)))

    def c_on(self, i, z, x):
        ref = self.slot(z, x, self.p.c)
        self.sent.append(push(ref, ref, self.cs, i, self.p.at(c=1 - self.p.c)))

    def wait(self, ref, sems, i):
        pltpu.make_async_remote_copy(
            src_ref=ref, dst_ref=ref, send_sem=sems[0].at[i], recv_sem=sems[1].at[i],
            device_id=self.p.at(c=1 - self.p.c), device_id_type=MESH,
        ).wait_recv()

    def from_z(self, k):
        p = self.p
        if k:
            self.wait(self.slot(p.back(k), p.x, p.c), self.zs, k)
            self.x_on(k)
            self.c_on(k, p.back(k), p.x)

    def from_x(self, k):
        p = self.p
        self.wait(self.slot(p.back(k), 1 - p.x, p.c), self.xs, k)
        self.c_on(p.depth + k, p.back(k), 1 - p.x)

    def near(self, k):
        p = self.p
        self.wait(self.slot(p.back(k), p.x, 1 - p.c), self.cs, k)

    def far(self, k):
        p = self.p
        self.wait(self.slot(p.back(k), 1 - p.x, 1 - p.c), self.cs, p.depth + k)

    def finish(self):
        for copy in self.sent:
            copy.wait_send()


def project_kernel(depth, attn, resid, w, gain, mid, normed, wbuf, act, rbuf, moving, landed, acc, *sems):
    ys, zs, xs, cs = [(sems[2 * i], sems[2 * i + 1]) for i in range(4)]
    p = Place(depth)
    g = lax.axis_index("groups")
    partner = {"groups": 1 - g}
    toks, feats = resid.shape
    rows, half = w.shape[0], feats // 2
    mine = pl.ds(pl.multiple_of(g * half, half), half)
    theirs = pl.ds(pl.multiple_of((1 - g) * half, half), half)

    def slot(z, x, c):
        return wbuf.at[z * 2 + x, pl.ds(pl.multiple_of(c * rows, rows), rows), :]

    greet(p.others() + [partner])
    wbuf[p.z * 2 + p.x, pl.ds(pl.multiple_of(p.c * rows, rows), rows), :] = w[:, mine]
    gather = Gather(p, slot, zs, xs, cs)
    gather.start()
    give = [
        push(attn, act.at[pl.ds(toks, toks), :], ys, 0, partner),
        push(resid.at[:, theirs], rbuf, ys, 1, partner),
    ]
    act[pl.ds(0, toks), :] = attn[...]
    acc[...] = jnp.zeros_like(acc)
    wide = tile(half, 256)

    def add(block):
        left = act[:, pl.ds(pl.multiple_of(block * 2 * rows, 2 * rows), 2 * rows)]

        def step(j, _):
            cols = pl.ds(pl.multiple_of(j * wide, wide), wide)
            acc[:, cols] += jnp.dot(left, wbuf[block, :, cols], preferred_element_type=F32)
            return 0

        lax.fori_loop(0, half // wide, step, 0)

    def both(k):
        if k == 0:
            for copy in give:
                copy.wait_recv()
        gather.near(k)
        add(p.back(k) * 2 + p.x)
        gather.far(k)
        add(p.back(k) * 2 + 1 - p.x)

    for k in range(depth):
        gather.from_z(k)
        gather.from_x(k)
        if k >= 2:
            both(k - 2)
    for k in range(max(depth - 2, 0), depth):
        both(k)

    moving[...] = (rbuf[...].astype(F32) + acc[pl.ds(toks, toks), :]).astype(BF16)
    back = push(moving, landed, ys, 2, partner)
    mid[:, mine] = (resid[:, mine].astype(F32) + acc[pl.ds(0, toks), :]).astype(BF16)
    back.wait_recv()
    mid[:, theirs] = landed[...]
    values = mid[...].astype(F32)
    mean_sq = jnp.sum(values * values, axis=-1, keepdims=True) * (1.0 / feats)
    normed[...] = (values * lax.rsqrt(mean_sq + epsilon) * gain[...]).astype(BF16)
    for copy in give + [back]:
        copy.wait_send()
    gather.finish()


def project(attn_heads, residual, w_out, gain, n):
    toks, feats = residual.shape
    rows, half = w_out.shape[0], feats // 2
    depth = n // 4
    vmem = pl.BlockSpec(memory_space=pltpu.VMEM)
    out = jax.ShapeDtypeStruct((toks, feats), BF16)
    counts = [3, 3, depth, depth, depth, depth, 2 * depth, 2 * depth]
    return pl.pallas_call(
        functools.partial(project_kernel, depth),
        out_shape=(out, out),
        in_specs=[vmem] * 4,
        out_specs=(vmem, vmem),
        scratch_shapes=[
            VM((2 * depth, 2 * rows, half), BF16),
            VM((2 * toks, attn_heads.shape[1]), BF16),
            VM((toks, half), BF16),
            VM((toks, half), BF16),
            VM((toks, half), BF16),
            VM((2 * toks, half), F32),
        ]
        + [DMA((count,)) for count in counts],
        compiler_params=pltpu.CompilerParams(collective_id=0, has_side_effects=True, vmem_limit_bytes=VMEM_BYTES),
        name="project",
    )(attn_heads, residual, w_out, gain)


def expert_kernel(
    depth, normed, share, wg_hbm, wu_hbm, wd_hbm, out,
    tok, part, cland, xland, zland, hidden, wg, wu, wd, load, *sems,
):
    zs, xs, cs, rz, rx, rc = [(sems[2 * i], sems[2 * i + 1]) for i in range(6)]
    p = Place(depth)
    toks, feats = normed.shape
    hid = wg.shape[1]
    mine = pl.ds(pl.multiple_of(p.c * toks, toks), toks)
    theirs = pl.ds(pl.multiple_of((1 - p.c) * toks, toks), toks)

    loads = [pltpu.make_async_copy(s, d, load.at[i]) for i, (s, d) in enumerate([(wg_hbm, wg), (wu_hbm, wu), (wd_hbm, wd)])]
    for copy in loads:
        copy.start()

    def slot(z, x, c):
        return tok.at[z * 2 + x, pl.ds(pl.multiple_of(c * toks, toks), toks), :]

    greet(p.others())
    tok[p.z * 2 + p.x, mine, :] = normed[...]
    gather = Gather(p, slot, zs, xs, cs)
    gather.start()
    sent = gather.sent
    wide_h, wide_d = tile(hid, 256), tile(feats, 256)

    def compute(block):
        def up(j, _):
            cols = pl.ds(pl.multiple_of(j * wide_h, wide_h), wide_h)
            gate = jnp.dot(tok[block], wg[:, cols], preferred_element_type=F32)
            lift = jnp.dot(tok[block], wu[:, cols], preferred_element_type=F32)
            hidden[:, cols] = (gate / (1.0 + jnp.exp(-gate)) * lift).astype(BF16)
            return 0

        def down(j, _):
            cols = pl.ds(pl.multiple_of(j * wide_d, wide_d), wide_d)
            y = jnp.dot(hidden[...], wd[:, cols], preferred_element_type=F32).astype(BF16)
            part[block, :, cols] = (y.astype(F32) * share[block]).astype(BF16)
            return 0

        lax.fori_loop(0, hid // wide_h, up, 0)
        lax.fori_loop(0, feats // wide_d, down, 0)

    core, across, along = {}, {}, {}

    def blocks(k):
        return p.back(k) * 2 + 1 - p.x, p.back(k) * 2 + p.x

    def first(k):
        far, near = blocks(k)
        gather.from_z(k)
        gather.from_x(k)
        if k == 0:
            for copy in loads:
                copy.wait()
        for i, block in ((depth + k, far), (k, near)):
            (gather.near if i < depth else gather.far)(k)
            compute(block)
            core[i] = push(part.at[block, theirs, :], cland.at[block], rc, i, p.at(c=1 - p.c))

    def add_to(block, ref):
        part[block, mine, :] = (part[block, mine, :].astype(F32) + ref.astype(F32)).astype(BF16)

    def second(k):
        far, near = blocks(k)
        core[depth + k].wait_recv()
        add_to(far, cland[far])
        across[k] = push(part.at[far, mine, :], xland.at[k], rx, k, p.at(x=1 - p.x))
        core[k].wait_recv()
        add_to(near, cland[near])

    def third(k):
        _, near = blocks(k)
        across[k].wait_recv()
        if k:
            add_to(near, xland[k])
            along[k] = push(part.at[near, mine, :], zland.at[k - 1], rz, k - 1, p.at(z=p.back(k)))

    for t in range(depth + 2):
        if t < depth:
            first(t)
        if 0 <= t - 1 < depth:
            second(t - 1)
        if 0 <= t - 2 < depth:
            third(t - 2)

    total = part[p.z * 2 + p.x, mine, :].astype(F32) + xland[0].astype(F32)
    for k in range(1, depth):
        along[k].wait_recv()
        total = total + zland[k - 1].astype(F32)
    out[...] = total.astype(BF16)
    for copy in list(core.values()) + list(across.values()) + list(along.values()):
        copy.wait_send()
    gather.finish()


def experts(normed, share, w_gate, w_up, w_down, n):
    toks, feats = normed.shape
    hid = w_gate.shape[1]
    depth = n // 4
    vmem = pl.BlockSpec(memory_space=pltpu.VMEM)
    hbm = pl.BlockSpec(memory_space=pl.ANY)
    lots = max(depth - 1, 1)
    counts = [depth, depth, depth, depth, 2 * depth, 2 * depth, lots, lots, depth, depth, 2 * depth, 2 * depth]
    return pl.pallas_call(
        functools.partial(expert_kernel, depth),
        out_shape=jax.ShapeDtypeStruct((toks, feats), BF16),
        in_specs=[vmem, vmem, hbm, hbm, hbm],
        out_specs=vmem,
        scratch_shapes=[
            VM((2 * depth, 2 * toks, feats), BF16),
            VM((2 * depth, 2 * toks, feats), BF16),
            VM((2 * depth, toks, feats), BF16),
            VM((depth, toks, feats), BF16),
            VM((lots, toks, feats), BF16),
            VM((2 * toks, hid), BF16),
            VM(w_gate.shape, BF16),
            VM(w_up.shape, BF16),
            VM(w_down.shape, BF16),
            DMA((3,)),
        ]
        + [DMA((count,)) for count in counts],
        compiler_params=pltpu.CompilerParams(collective_id=1, has_side_effects=True, vmem_limit_bytes=VMEM_BYTES),
        name="experts",
    )(normed, share, w_gate, w_up, w_down)


def dense(attn_heads, residual, w_out, norm_gain, expert_ids, route_num, w_gate, w_up, w_down):
    n = lax.axis_size("expert")
    toks = residual.shape[0]
    numer = route_num.astype(F32)
    weights = numer / jnp.sum(numer, axis=1, keepdims=True)
    chosen = expert_ids[:, :, None] == jnp.arange(n, dtype=jnp.int32)[None, None, :]
    table = jnp.sum(jnp.where(chosen, weights[:, :, None], 0.0), axis=1)
    tables = lax.all_gather(table.T, "expert", axis=0)
    share = lax.dynamic_index_in_dim(tables, lax.axis_index("expert"), axis=1, keepdims=False)
    share = share.reshape(n // 2, 2 * toks, 1)
    mid_state, normed = project(attn_heads, residual, w_out, norm_gain[None, :], n)
    return mid_state, experts(normed, share, w_gate[0], w_up[0], w_down[0], n)


def sparse(attn_heads, residual, w_out, norm_gain, expert_ids, route_num, w_gate, w_up, w_down):
    tok_rows = attn_heads.shape[0]
    feature_count = residual.shape[1]
    gathered = lax.all_gather(w_out, "expert", axis=0, tiled=True)
    projected = jnp.dot(attn_heads, gathered, preferred_element_type=F32)
    mid_state = (residual.astype(F32) + projected).astype(BF16)
    n_experts = lax.axis_size("expert")
    top_count = expert_ids.shape[1]
    capacity = tok_rows * top_count * 5 // (4 * n_experts)
    onehot = expert_ids[:, :, None] == jnp.arange(n_experts, dtype=jnp.int32)[None, None, :]
    order = jnp.arange(tok_rows, dtype=jnp.int32)
    earlier = (order[:, None] > order[None, :]).astype(BF16)
    before = jnp.dot(earlier, jnp.any(onehot, axis=1).astype(BF16), preferred_element_type=F32)
    slot_index = jnp.sum(jnp.where(onehot, before[:, None, :], 0.0), axis=2).astype(jnp.int32)
    position = expert_ids * capacity + slot_index
    payload = rms_scale(mid_state, norm_gain)
    spots = jnp.arange(n_experts * capacity, dtype=jnp.int32)
    pick = jnp.any(position[None] == spots[:, None, None], axis=2).astype(BF16)
    sendbuf = jnp.dot(pick, payload, preferred_element_type=F32).astype(BF16)
    sendbuf = sendbuf.reshape(n_experts, capacity, feature_count)
    received = lax.all_to_all(sendbuf, "expert", split_axis=0, concat_axis=0, tiled=True)
    sources, slot_count, _ = received.shape
    row_block = received.reshape(sources * slot_count, feature_count)
    gate_act = jnp.dot(row_block, w_gate[0], preferred_element_type=F32)
    up_act = jnp.dot(row_block, w_up[0], preferred_element_type=F32)
    hidden = (jax.nn.silu(gate_act) * up_act).astype(BF16)
    result = jnp.dot(hidden, w_down[0], preferred_element_type=F32).astype(BF16)
    result = result.reshape(sources, slot_count, feature_count)
    returned = lax.all_to_all(result, "expert", split_axis=0, concat_axis=0, tiled=True)
    returned = returned.reshape(n_experts * capacity, feature_count)
    numer = route_num.astype(F32)
    weights = numer / jnp.sum(numer, axis=1, keepdims=True)
    hit = position[:, :, None] == spots[None, None, :]
    blend = jnp.sum(jnp.where(hit, weights[:, :, None], 0.0), axis=1)
    expert_out = jnp.dot(blend, returned.astype(F32), precision=lax.Precision.HIGHEST).astype(BF16)
    return (mid_state, expert_out)


def solution(mesh):
    n, groups = mesh.shape["expert"], mesh.shape["groups"]
    in_specs = (
        P(("groups", "expert"), None),
        P(("groups", "expert"), None),
        P("expert", None),
        P(),
        P(("groups", "expert"), None),
        P(("groups", "expert"), None),
        P("expert", None, None),
        P("expert", None, None),
        P("expert", None, None),
    )
    out_specs = (P(("groups", "expert"), None), P(("groups", "expert"), None))

    def per_device(*args):
        residual, w_out, ids, w_gate = args[1], args[2], args[4], args[6]
        toks, feats = residual.shape
        held = 2 * feats * (toks * (3 * n + n // 2) + 3 * w_gate.shape[2])
        few = n <= 2 * ids.shape[1] and held <= VMEM_BYTES * 3 // 4
        even = n % 4 == 0 and groups == 2 and feats % 256 == 0 and w_out.shape[0] % 64 == 0 and toks % 16 == 0
        return (dense if few and even else sparse)(*args)

    return jax.shard_map(per_device, mesh=mesh, in_specs=in_specs, out_specs=out_specs, check_vma=False)
```

time: 454 us -> 292 us (0.64)
  Pallas kernels: 0 us -> 258 us
  waiting for transfers between devices: 230 us -> 0 us
  blocking collectives: 120 us -> 20.7 us
  local copies, waits for them, and re-layouts: 38.1 us -> 4.57 us
  matrix products: 23.8 us -> 0 us
  between operations: 14.2 us -> 0.66 us
  other arithmetic: 13.7 us -> 2.1 us
  starting transfers between devices: 6.16 us -> 0 us
    pallas_call x0 -> x2, Pallas kernels: none -> 258 us  [the longest x1 173 us: experts(): pl.pallas_call(functools.partial(expert_kernel, depth), out_shape=jax.Sha...]
    all_gather x1 -> x0, waiting for transfers between devices: 122 us -> none  [per_device(): gathered = lax.all_gather(w_out, 'expert', axis=0, tiled=True)]
    all_to_all x1 -> x0, blocking collectives: 120 us -> none  [per_device(): lax.all_to_all(sendbuf, 'expert', split_axis=0, concat_axis=0, tiled=True)]
    all_to_all x1 -> x0, waiting for transfers between devices: 107 us -> none  [per_device(): lax.all_to_all(result, 'expert', split_axis=0, concat_axis=0, tiled=True)]
    dot_general x4 -> x0, matrix products: 23.8 us -> none  [the longest x1 8.6 us: per_device(): jnp.dot(attn_heads, gathered, preferred_element_type=jnp.float32)]
    scatter x1 -> x0, local copies, waits for them, and re-layouts: 23.5 us -> none  [per_device(): sendbuf = sendbuf.at[position].set(payload[token_index])]
    all_gather x0 -> x1, blocking collectives: none -> 20.7 us  [dense(): tables = lax.all_gather(table.T, 'expert', axis=0)]
    gather x1 -> x0, local copies, waits for them, and re-layouts: 12 us -> none  [per_device(): returned[position].astype(jnp.float32)]
  transfers between devices with their start and end apart: 2 -> 0, of which waited for: 2 -> 0; matrix products, arithmetic and copies ran while one was open for 2% -> 0% of each run, Pallas kernels for 0% -> 0%
where the time goes in v1:
time: 292 us; the launch traced here: 286 us
  Pallas kernels  258 us (88%)
  blocking collectives  20.7 us (7%)
  local copies, waits for them, and re-layouts  4.57 us (2%)
    pallas_call x1, Pallas kernels, experts(): pl.pallas_call(functools.partial(expert_kernel, depth), out_shape=jax.Sha...  173 us
    pallas_call x1, Pallas kernels, project(): pl.pallas_call(functools.partial(project_kernel, depth), out_shape=(out,...  85.7 us
    all_gather x1, blocking collectives, dense(): tables = lax.all_gather(table.T, 'expert', axis=0)  20.7 us

profile of v1, /device:TPU:25, one launch (start us, length us, event | category | flops | bytes accessed | tf_op | source)
XLA Modules:
  0.0 286.2 jit_solution(539588451083364376)
XLA Ops:
  0.6 85.7 %project.1 = (bf16[128,2048]{1,0:T(8,128)(2,1)}, bf16[128,2048]{1,0:T(8,128)(2,1)}) custom-call(bf16[128,4096]{1,0:T(8,128)(2,1)} %attn.1, bf16[128,2048]{1,0:T(8,128)(2,1)} %resid.1, bf16[256,2048]{1,0:T(8,128)(2,1)} %w.1, f32[1,2048]{1,0:T(1,128)} %bitcast.11), custom_call_target="tpu_custom_call" | custom-call | tf_op jit(solution)/shard_map/project/pallas_call | solution.py:188
  86.4 0.7 convert_reduce_fusion
  87.1 0.7 convert_divide_fusion
  87.8 0.7 select_reduce_fusion
  88.5 20.7 %all-gather = f32[256,128]{1,0:T(8,128)S(1)} all-gather(f32[16,128]{1,0:T(8,128)S(1)} %bitcast.10), channel_id=2, replica_groups=mesh['groups'=2,'expert'=16] {'expert'}, dimensions={0}, use_global_device_ids=true | all-gather | bytes 139264 | tf_op jit(solution)/shard_map/all_gather | solution.py:340
  109.2 1.9 reshape.13.share
  111.0 0.0 copy-start
  111.0 172.5 %experts.1 = bf16[128,2048]{1,0:T(8,128)(2,1)} custom-call(bf16[128,2048]{1,0:T(8,128)(2,1)} %get-tuple-element.5.normed, f32[8,256,1]{2,1,0:T(8,128)} %reshape.13.share, bf16[2048,768]{1,0:T(8,128)(2,1)} %bitcast.6, bf16[2048,768]{1,0:T(8,128)(2,1)} %bitcast.7, bf16[768,2048]{1,0:T(8,128)(2,1)} %bitcast.8), custom_call_target="tpu_custom_call" | custom-call | tf_op jit(solution)/shard_map/experts/pallas_call | solution.py:310
  283.6 0.0 copy-done
  283.6 0.8 copy.19
  284.4 1.9 copy.20
  (1 shorter events, 0.0 us)
Async XLA Ops:
  111.0 172.5 %copy-start = (bf16[128,2048]{1,0:T(8,128)(2,1)S(1)}, bf16[128,2048]{1,0:T(8,128)(2,1)}, u32[]{:S(2)}) copy-start(bf16[128,2048]{1,0:T(8,128)(2,1)} %get-tuple-element.8) | copy-start | bytes 1572868

commit v2 on v1

--- a/solution.py
+++ b/solution.py
@@ -30,8 +30,14 @@
         self.depth = depth
         self.z, self.x, self.c = e // 4, (e // 2) % 2, e % 2
 
-    def back(self, k):
-        return lax.rem(self.z + self.depth - k, self.depth)
+    def source(self, k):
+        if k == 0:
+            return self.z
+        above = self.depth - 1 - self.z
+        near = jnp.minimum(self.z, above)
+        level = self.z - (k + 1) // 2 if k % 2 else self.z + k // 2
+        beyond = jnp.where(self.z < above, self.z + k - near, self.z - k + near)
+        return jnp.where(k <= 2 * near, level, beyond)
 
     def at(self, z=None, x=None, c=None):
         z = self.z if z is None else z
@@ -60,61 +66,67 @@
 
 
 class Gather:
-    def __init__(self, place, slot, zs, xs, cs):
-        self.p, self.slot, self.zs, self.xs, self.cs = place, slot, zs, xs, cs
-        self.sent = []
-
-    def start(self):
+    def __init__(self, place, slot, up, down, across, core):
+        self.p, self.slot, self.up, self.down, self.across, self.core = place, slot, up, down, across, core
+        self.sources = [place.source(k) for k in range(place.depth)]
+
+    def copy(self, z, x, c, sems, i, target):
+        ref = self.slot(z, x, c)
+        return pltpu.make_async_remote_copy(
+            src_ref=ref, dst_ref=ref, send_sem=sems[0].at[i], recv_sem=sems[1].at[i],
+            device_id=target, device_id_type=MESH,
+        )
+
+    def hops(self, z):
         p = self.p
-        own = self.slot(p.z, p.x, p.c)
-        self.landed = {}
-        for k in range(1, p.depth):
-            self.sent.append(push(own, own, self.zs, k, p.at(z=lax.rem(p.z + k, p.depth))))
-        self.x_on(0)
-        self.c_on(0, p.z, p.x)
-
-    def x_on(self, k):
+        up = self.copy(z, p.x, p.c, self.up, z, p.at(z=jnp.minimum(p.z + 1, p.depth - 1)))
+        down = self.copy(z, p.x, p.c, self.down, z, p.at(z=jnp.maximum(p.z - 1, 0)))
+        return ((z <= p.z) & (p.z < p.depth - 1), up), ((z >= p.z) & (p.z > 0), down)
+
+    def others(self, z):
         p = self.p
-        ref = self.slot(p.back(k), p.x, p.c)
-        self.sent.append(push(ref, ref, self.xs, k, p.at(x=1 - p.x)))
-
-    def c_on(self, i, z, x):
-        ref = self.slot(z, x, self.p.c)
-        self.sent.append(push(ref, ref, self.cs, i, self.p.at(c=1 - self.p.c)))
-
-    def wait(self, ref, sems, i):
-        pltpu.make_async_remote_copy(
-            src_ref=ref, dst_ref=ref, send_sem=sems[0].at[i], recv_sem=sems[1].at[i],
-            device_id=self.p.at(c=1 - self.p.c), device_id_type=MESH,
-        ).wait_recv()
+        over = self.copy(z, p.x, p.c, self.across, z, p.at(x=1 - p.x))
+        near = self.copy(z, p.x, p.c, self.core, z, p.at(c=1 - p.c))
+        far = self.copy(z, 1 - p.x, p.c, self.core, p.depth + z, p.at(c=1 - p.c))
+        return over, near, far
 
     def from_z(self, k):
-        p = self.p
+        p, z = self.p, self.sources[k]
         if k:
-            self.wait(self.slot(p.back(k), p.x, p.c), self.zs, k)
-            self.x_on(k)
-            self.c_on(k, p.back(k), p.x)
+            up, down = [copy for _, copy in self.hops(z)]
+            pl.when(z < p.z)(up.wait_recv)
+            pl.when(z > p.z)(down.wait_recv)
+        for made, copy in self.hops(z):
+            pl.when(made)(copy.start)
+        over, near, _ = self.others(z)
+        over.start()
+        near.start()
 
     def from_x(self, k):
-        p = self.p
-        self.wait(self.slot(p.back(k), 1 - p.x, p.c), self.xs, k)
-        self.c_on(p.depth + k, p.back(k), 1 - p.x)
+        p, z = self.p, self.sources[k]
+        self.copy(z, 1 - p.x, p.c, self.across, z, p.at(x=1 - p.x)).wait_recv()
+        self.others(z)[2].start()
 
     def near(self, k):
-        p = self.p
-        self.wait(self.slot(p.back(k), p.x, 1 - p.c), self.cs, k)
+        p, z = self.p, self.sources[k]
+        self.copy(z, p.x, 1 - p.c, self.core, z, p.at(c=1 - p.c)).wait_recv()
 
     def far(self, k):
-        p = self.p
-        self.wait(self.slot(p.back(k), 1 - p.x, 1 - p.c), self.cs, p.depth + k)
+        p, z = self.p, self.sources[k]
+        self.copy(z, 1 - p.x, 1 - p.c, self.core, p.depth + z, p.at(c=1 - p.c)).wait_recv()
 
     def finish(self):
-        for copy in self.sent:
-            copy.wait_send()
-
-
-def project_kernel(depth, attn, resid, w, gain, mid, normed, wbuf, act, rbuf, moving, landed, acc, *sems):
-    ys, zs, xs, cs = [(sems[2 * i], sems[2 * i + 1]) for i in range(4)]
+        for z in self.sources:
+            for made, copy in self.hops(z):
+                pl.when(made)(copy.wait_send)
+            for copy in self.others(z):
+                copy.wait_send()
+
+
+def project_kernel(
+    depth, attn, resid, w, gain, table, mid, normed, share, wbuf, act, rbuf, moving, landed, acc, tables, *sems
+):
+    ys, us, ds, xs, cs, tu, td, tx, tc = [(sems[2 * i], sems[2 * i + 1]) for i in range(9)]
     p = Place(depth)
     g = lax.axis_index("groups")
     partner = {"groups": 1 - g}
@@ -128,8 +140,11 @@
 
     greet(p.others() + [partner])
     wbuf[p.z * 2 + p.x, pl.ds(pl.multiple_of(p.c * rows, rows), rows), :] = w[:, mine]
-    gather = Gather(p, slot, zs, xs, cs)
-    gather.start()
+    tables[(p.z * 2 + p.x) * 2 + p.c] = table[...]
+    routes = Gather(p, lambda z, x, c: tables.at[(z * 2 + x) * 2 + c], tu, td, tx, tc)
+    routes.from_z(0)
+    gather = Gather(p, slot, us, ds, xs, cs)
+    gather.from_z(0)
     give = [
         push(attn, act.at[pl.ds(toks, toks), :], ys, 0, partner),
         push(resid.at[:, theirs], rbuf, ys, 1, partner),
@@ -153,20 +168,27 @@
             for copy in give:
                 copy.wait_recv()
         gather.near(k)
-        add(p.back(k) * 2 + p.x)
+        add(gather.sources[k] * 2 + p.x)
         gather.far(k)
-        add(p.back(k) * 2 + 1 - p.x)
-
-    for k in range(depth):
-        gather.from_z(k)
-        gather.from_x(k)
-        if k >= 2:
-            both(k - 2)
+        add(gather.sources[k] * 2 + 1 - p.x)
+
+    for k in range(1, depth + 1):
+        if k < depth:
+            routes.from_z(k)
+            gather.from_z(k)
+        routes.from_x(k - 1)
+        gather.from_x(k - 1)
+        if k >= 3:
+            both(k - 3)
     for k in range(max(depth - 2, 0), depth):
         both(k)
 
     moving[...] = (rbuf[...].astype(F32) + acc[pl.ds(toks, toks), :]).astype(BF16)
     back = push(moving, landed, ys, 2, partner)
+    for k in range(depth):
+        routes.near(k)
+        routes.far(k)
+    share[...] = tables[:, lax.axis_index("expert"), :]
     mid[:, mine] = (resid[:, mine].astype(F32) + acc[pl.ds(0, toks), :]).astype(BF16)
     back.wait_recv()
     mid[:, theirs] = landed[...]
@@ -176,20 +198,21 @@
     for copy in give + [back]:
         copy.wait_send()
     gather.finish()
-
-
-def project(attn_heads, residual, w_out, gain, n):
+    routes.finish()
+
+
+def project(attn_heads, residual, w_out, gain, table, n):
     toks, feats = residual.shape
     rows, half = w_out.shape[0], feats // 2
     depth = n // 4
     vmem = pl.BlockSpec(memory_space=pltpu.VMEM)
     out = jax.ShapeDtypeStruct((toks, feats), BF16)
-    counts = [3, 3, depth, depth, depth, depth, 2 * depth, 2 * depth]
+    counts = [3, 3] + 2 * (6 * [depth] + 2 * [2 * depth])
     return pl.pallas_call(
         functools.partial(project_kernel, depth),
-        out_shape=(out, out),
-        in_specs=[vmem] * 4,
-        out_specs=(vmem, vmem),
+        out_shape=(out, out, jax.ShapeDtypeStruct((n, toks), F32)),
+        in_specs=[vmem] * 5,
+        out_specs=(vmem, vmem, vmem),
         scratch_shapes=[
             VM((2 * depth, 2 * rows, half), BF16),
             VM((2 * toks, attn_heads.shape[1]), BF16),
@@ -197,18 +220,19 @@
             VM((toks, half), BF16),
             VM((toks, half), BF16),
             VM((2 * toks, half), F32),
+            VM((n,) + table.shape, F32),
         ]
         + [DMA((count,)) for count in counts],
         compiler_params=pltpu.CompilerParams(collective_id=0, has_side_effects=True, vmem_limit_bytes=VMEM_BYTES),
         name="project",
-    )(attn_heads, residual, w_out, gain)
+    )(attn_heads, residual, w_out, gain, table)
 
 
 def expert_kernel(
     depth, normed, share, wg_hbm, wu_hbm, wd_hbm, out,
     tok, part, cland, xland, zland, hidden, wg, wu, wd, load, *sems,
 ):
-    zs, xs, cs, rz, rx, rc = [(sems[2 * i], sems[2 * i + 1]) for i in range(6)]
+    us, ds, xs, cs, rz, rx, rc = [(sems[2 * i], sems[2 * i + 1]) for i in range(7)]
     p = Place(depth)
     toks, feats = normed.shape
     hid = wg.shape[1]
@@ -224,9 +248,8 @@
 
     greet(p.others())
     tok[p.z * 2 + p.x, mine, :] = normed[...]
-    gather = Gather(p, slot, zs, xs, cs)
-    gather.start()
-    sent = gather.sent
+    gather = Gather(p, slot, us, ds, xs, cs)
+    gather.from_z(0)
     wide_h, wide_d = tile(hid, 256), tile(feats, 256)
 
     def compute(block):
@@ -246,40 +269,55 @@
         lax.fori_loop(0, hid // wide_h, up, 0)
         lax.fori_loop(0, feats // wide_d, down, 0)
 
-    core, across, along = {}, {}, {}
+    core, across = {}, {}
 
     def blocks(k):
-        return p.back(k) * 2 + 1 - p.x, p.back(k) * 2 + p.x
+        z = gather.sources[k]
+        return z * 2 + 1 - p.x, z * 2 + p.x
 
     def first(k):
         far, near = blocks(k)
-        gather.from_z(k)
+        if k + 1 < depth:
+            gather.from_z(k + 1)
         gather.from_x(k)
         if k == 0:
             for copy in loads:
                 copy.wait()
-        for i, block in ((depth + k, far), (k, near)):
-            (gather.near if i < depth else gather.far)(k)
+        for name, block in (("far", far), ("near", near)):
+            (gather.far if name == "far" else gather.near)(k)
             compute(block)
-            core[i] = push(part.at[block, theirs, :], cland.at[block], rc, i, p.at(c=1 - p.c))
+            core[name, k] = push(part.at[block, theirs, :], cland.at[block], rc, block, p.at(c=1 - p.c))
 
     def add_to(block, ref):
         part[block, mine, :] = (part[block, mine, :].astype(F32) + ref.astype(F32)).astype(BF16)
 
     def second(k):
         far, near = blocks(k)
-        core[depth + k].wait_recv()
+        core["far", k].wait_recv()
         add_to(far, cland[far])
-        across[k] = push(part.at[far, mine, :], xland.at[k], rx, k, p.at(x=1 - p.x))
-        core[k].wait_recv()
+        z = gather.sources[k]
+        across[k] = push(part.at[far, mine, :], xland.at[z], rx, z, p.at(x=1 - p.x))
+        core["near", k].wait_recv()
         add_to(near, cland[near])
+
+    def along_to(k):
+        dest = lax.rem(p.z + k, depth)
+        return pltpu.make_async_remote_copy(
+            src_ref=part.at[dest * 2 + p.x, mine, :], dst_ref=zland.at[k - 1], send_sem=rz[0].at[k - 1],
+            recv_sem=rz[1].at[k - 1], device_id=p.at(z=dest), device_id_type=MESH,
+        )
 
     def third(k):
         _, near = blocks(k)
         across[k].wait_recv()
         if k:
-            add_to(near, xland[k])
-            along[k] = push(part.at[near, mine, :], zland.at[k - 1], rz, k - 1, p.at(z=p.back(k)))
+            z = gather.sources[k]
+            add_to(near, xland[z])
+            by = lax.rem(z - p.z + depth, depth)
+            pltpu.make_async_remote_copy(
+                src_ref=part.at[near, mine, :], dst_ref=zland.at[by - 1], send_sem=rz[0].at[by - 1],
+                recv_sem=rz[1].at[by - 1], device_id=p.at(z=z), device_id_type=MESH,
+            ).start()
 
     for t in range(depth + 2):
         if t < depth:
@@ -289,12 +327,12 @@
         if 0 <= t - 2 < depth:
             third(t - 2)
 
-    total = part[p.z * 2 + p.x, mine, :].astype(F32) + xland[0].astype(F32)
+    total = part[p.z * 2 + p.x, mine, :].astype(F32) + xland[p.z].astype(F32)
     for k in range(1, depth):
-        along[k].wait_recv()
+        along_to(k).wait_recv()
         total = total + zland[k - 1].astype(F32)
     out[...] = total.astype(BF16)
-    for copy in list(core.values()) + list(across.values()) + list(along.values()):
+    for copy in list(core.values()) + list(across.values()) + [along_to(k) for k in range(1, depth)]:
         copy.wait_send()
     gather.finish()
 
@@ -306,7 +344,7 @@
     vmem = pl.BlockSpec(memory_space=pltpu.VMEM)
     hbm = pl.BlockSpec(memory_space=pl.ANY)
     lots = max(depth - 1, 1)
-    counts = [depth, depth, depth, depth, 2 * depth, 2 * depth, lots, lots, depth, depth, 2 * depth, 2 * depth]
+    counts = 6 * [depth] + 2 * [2 * depth] + 2 * [lots] + 2 * [depth] + 2 * [2 * depth]
     return pl.pallas_call(
         functools.partial(expert_kernel, depth),
         out_shape=jax.ShapeDtypeStruct((toks, feats), BF16),
@@ -337,10 +375,8 @@
     weights = numer / jnp.sum(numer, axis=1, keepdims=True)
     chosen = expert_ids[:, :, None] == jnp.arange(n, dtype=jnp.int32)[None, None, :]
     table = jnp.sum(jnp.where(chosen, weights[:, :, None], 0.0), axis=1)
-    tables = lax.all_gather(table.T, "expert", axis=0)
-    share = lax.dynamic_index_in_dim(tables, lax.axis_index("expert"), axis=1, keepdims=False)
+    mid_state, normed, share = project(attn_heads, residual, w_out, norm_gain[None, :], table.T, n)
     share = share.reshape(n // 2, 2 * toks, 1)
-    mid_state, normed = project(attn_heads, residual, w_out, norm_gain[None, :], n)
     return mid_state, experts(normed, share, w_gate[0], w_up[0], w_down[0], n)
 
 

time: 292 us -> 210 us (0.72); the launches traced: 286 us -> 210 us
  Pallas kernels: 258 us -> 201 us
  blocking collectives: 20.7 us -> 0 us
    pallas_call x1, Pallas kernels: 173 us -> 139 us  [experts(): pl.pallas_call(functools.partial(expert_kernel, depth), out_shape=jax.Sha...]
    pallas_call x1, Pallas kernels: 85.7 us -> 61.5 us  [project(): pl.pallas_call(functools.partial(project_kernel, depth), out_shape=(out,...]
    all_gather x1 -> x0, blocking collectives: 20.7 us -> none  [dense(): tables = lax.all_gather(table.T, 'expert', axis=0)]
where the time goes in v2:
time: 210 us
  Pallas kernels  201 us (96%)
  local copies, waits for them, and re-layouts  5.24 us (2%)
  other arithmetic  2.7 us (1%)
    pallas_call x1, Pallas kernels, experts(): pl.pallas_call(functools.partial(expert_kernel, depth), out_shape=jax.Sha...  139 us
    pallas_call x1, Pallas kernels, project(): pl.pallas_call(functools.partial(project_kernel, depth), out_shape=(out,...  61.5 us

profile of v2, /device:TPU:25, one launch (start us, length us, event | category | flops | bytes accessed | tf_op | source)
XLA Modules:
  0.0 209.5 jit_solution(15857820636567428888)
XLA Ops:
  0.6 0.7 convert_reduce_fusion
  1.3 0.7 convert_divide_fusion
  2.0 1.3 select_reduce_fusion
  3.3 61.5 %project.1 = (bf16[128,2048]{1,0:T(8,128)(2,1)}, bf16[128,2048]{1,0:T(8,128)(2,1)}, f32[16,128]{1,0:T(8,128)}) custom-call(bf16[128,4096]{1,0:T(8,128)(2,1)} %attn.1, bf16[128,2048]{1,0:T(8,128)(2,1)} %resid.1, bf16[256,2048]{1,0:T(8,128)(2,1)} %w.1, f32[1,2048]{1,0:T(1,128)} %bitcast.9, f32[16,128]{1,0:T(8,128)} %bitcast.8), custom_call_target="tpu_custom_call" | custom-call | tf_op jit(solution)/shard_map/project/pallas_call | solution.py:211
  64.8 2.6 %reshape.11.share = f32[8,256,1]{2,1,0:T(8,128)} reshape(f32[16,128]{1,0:T(8,128)} %get-tuple-element.7) | data formatting | bytes 16384 | tf_op jit(solution)/shard_map/reshape | solution.py:379
  67.4 0.0 copy-start
  67.4 139.5 %experts.1 = bf16[128,2048]{1,0:T(8,128)(2,1)} custom-call(bf16[128,2048]{1,0:T(8,128)(2,1)} %get-tuple-element.6.normed, f32[8,256,1]{2,1,0:T(8,128)} %reshape.11.share, bf16[2048,768]{1,0:T(8,128)(2,1)} %bitcast.5, bf16[2048,768]{1,0:T(8,128)(2,1)} %bitcast.6, bf16[768,2048]{1,0:T(8,128)(2,1)} %bitcast.7), custom_call_target="tpu_custom_call" | custom-call | tf_op jit(solution)/shard_map/experts/pallas_call | solution.py:348
  206.9 0.0 copy-done
  206.9 0.8 copy.19
  207.7 1.9 copy.20
Async XLA Ops:
  67.4 139.5 %copy-start = (bf16[128,2048]{1,0:T(8,128)(2,1)S(1)}, bf16[128,2048]{1,0:T(8,128)(2,1)}, u32[]{:S(2)}) copy-start(bf16[128,2048]{1,0:T(8,128)(2,1)} %get-tuple-element.10) | copy-start | bytes 1572868
